TPU v7x, 128 devices: a whole 4x4x4 slice. The times are simulated.
128 devices in a mesh: scene: 4 (over y), tile: 32 (over x, z, core).
Axes of the slice: x: 4, y: 4, z: 4, core: 2. Of those that a mesh axis runs over, the one named last changes fastest.
Arguments:
- features: bfloat16 [128, 32, 64, 768], P(('scene', 'tile')), parts along dimension 0, may hold values from -120 to 120
- dw_kernel: bfloat16 [3, 3, 3, 768], replicated, may hold values from -2 to 2
- se_reduce: bfloat16 [3, 768, 192], replicated, may hold values from -0.21875 to 0.21875
- se_expand: bfloat16 [3, 192, 768], replicated, may hold values from -0.4375 to 0.4375
- mix_weight: bfloat16 [3, 768, 768], replicated, may hold values from -0.21875 to 0.21875
- norm_gain: float32 [768], replicated, may hold values from 0.5 to 2
- kv_weight: bfloat16 [768, 1536], replicated, may hold values from -0.21875 to 0.21875
- kv_bias: float32 [1536], replicated, may hold values from -3 to 3
- proj_weight: bfloat16 [768, 768], replicated, may hold values from -0.21875 to 0.21875
- proj_bias: float32 [768], replicated, may hold values from -3 to 3
Outputs:
- blocked: bfloat16 [128, 32, 64, 768], P(('scene', 'tile')), parts along dimension 0
There are 4 independent parts, one for each index of `scene`. A program takes and returns all parts, laid end to end along the dimension named above; an argument that names none is the same for every part. Nothing has to cross between parts.
All inputs are finite; a program needn't handle non-finite values.
Results may differ from a plain program's by a relative error of at most 0.008.
The roundings to bfloat16 on the way count: a program that leaves them out, or rounds other values in their place, can miss the bound.
Values may be sent and summed in bfloat16 or wider, within the bound.
No kernel may reach another device: no remote copies, remote signals or barrier semaphores. Data moves between devices by JAX's collectives and lax.ppermute only.
A program may use at most 128 MiB of HBM per device.

v0:
```python
import functools

import jax
import jax.numpy as jnp
from jax import lax
from jax.experimental import pallas as pl
from jax.experimental.pallas import tpu as pltpu
from jax.sharding import PartitionSpec as P

HEADS = 24
TILE_COLS = 4
EPSILON = 1e-05
BF = jnp.bfloat16
F32 = jnp.float32
VM = pl.BlockSpec(memory_space=pltpu.VMEM)
LOG2E = 1.4426950408889634
QB = 256
KC = 512
UNROLL = {1: 4, 2: 8, 3: 8}


def kv_kernel(x_ref, gain_ref, w_ref, b_ref, kt_ref, vt_ref):
    dim = x_ref.shape[-1]
    tokens = x_ref.shape[0] * x_ref.shape[1]
    x = x_ref[...].reshape(tokens, dim).astype(F32)
    centre = jnp.mean(x, axis=1, keepdims=True)
    moved = x - centre
    spread = jnp.mean(jnp.square(moved), axis=1, keepdims=True)
    normed = (moved * lax.rsqrt(spread + EPSILON) * gain_ref[...].reshape(1, dim)).astype(BF)
    keys = (jnp.dot(normed, w_ref[:, :dim], preferred_element_type=F32) + b_ref[:dim].reshape(1, dim)).astype(BF)
    for group in range(dim // 128):
        kt_ref[group] = keys[:, 128 * group : 128 * group + 128]
    vals = jnp.dot(normed, w_ref[:, dim:], preferred_element_type=F32) + b_ref[dim:].reshape(1, dim)
    vt_ref[...] = vals.T.astype(BF)


def keys_values(tile_map, gain, weight, bias, window):
    win, _, dim = tile_map.shape
    step = 8
    tokens = step * win
    return pl.pallas_call(
        kv_kernel,
        grid=(win // step,),
        in_specs=[
            pl.BlockSpec((step, win, dim), lambda i: (i, window, 0)),
            pl.BlockSpec((dim,), lambda i: (0,)),
            pl.BlockSpec((dim, 2 * dim), lambda i: (0, 0)),
            pl.BlockSpec((2 * dim,), lambda i: (0,)),
        ],
        out_specs=[
            pl.BlockSpec((dim // 128, tokens, 128), lambda i: (0, i, 0)),
            pl.BlockSpec((dim, tokens), lambda i: (0, i)),
        ],
        out_shape=[
            jax.ShapeDtypeStruct((dim // 128, win * win, 128), BF),
            jax.ShapeDtypeStruct((dim, win * win), BF),
        ],
        compiler_params=pltpu.CompilerParams(vmem_limit_bytes=24 * 2**20),
        cost_estimate=pl.CostEstimate(
            flops=8 * win * win * dim * dim, bytes_accessed=8 * 2**20, transcendentals=0
        ),
        name="keys_values",
    )(tile_map, gain, weight, bias)


def attention_kernel(steps, *refs):
    slabs = len(steps)
    q_refs = refs[:slabs]
    kt_refs, vt_refs = refs[slabs : slabs + 2], refs[slabs + 2 : slabs + 4]
    x_ref, wp_ref, bp_ref = refs[slabs + 4 : slabs + 7]
    out_ref, qa, sb, mb, ot, stage, sems = refs[-7:]
    dim = x_ref.shape[2]
    length = kt_refs[0].shape[1]
    units = HEADS * slabs
    unroll = UNROLL[slabs]
    scale = (dim // HEADS) ** (-0.5) * LOG2E
    lane = lax.broadcasted_iota(jnp.int32, (1, 128), 1)
    for slab in range(slabs):
        for group in range(dim // 128):
            q = q_refs[slab][:, 128 * group : 128 * group + 128]
            for part in range(4):
                qa[slab, 4 * group + part] = jnp.where(lane // 32 == part, q, jnp.zeros_like(q))
    ones = jnp.ones((16, KC), BF)

    def score(unit, slot, w, start):
        head = unit // slabs
        s = lax.dot_general(
            kt_refs[w][head // 4, pl.ds(start, KC), :],
            qa[unit % slabs, head],
            (((1,), (1,)), ((), ())),
            preferred_element_type=F32,
        )
        sb[slot, w, pl.ds(start, KC), :] = s
        return jnp.max(s.reshape(KC // 8, 8, QB), axis=0)

    def step(unit, slot, following):
        if unit is not None:
            head = unit // slabs
            rows = pl.ds(pl.multiple_of(head * 32, 32), 32)
        for w in range(2):
            top = total = None
            if unit is not None:
                peak = jnp.max(mb[slot, w], axis=0, keepdims=True)
            for start in range(0, length, KC):
                high = score(following, 1 - slot, w, start)
                top = high if top is None else jnp.maximum(top, high)
                if unit is not None:
                    p = jnp.exp2((sb[slot, w, pl.ds(start, KC), :] - peak) * scale).astype(BF)
                    v = jnp.concatenate([vt_refs[w][rows, pl.ds(start, KC)], ones], axis=0)
                    o = jnp.dot(v, p, preferred_element_type=F32)
                    total = o if total is None else total + o
            mb[1 - slot, w] = top
            if unit is not None:
                ot[unit % slabs, w, rows, :] = (total[:32] / total[32:33]).astype(BF)

    step(None, 1, 0)

    def body(turn, _):
        for j in range(unroll):
            unit = unroll * turn + j
            step(unit, j % 2, jnp.minimum(unit + 1, units - 1))
        return 0

    lax.fori_loop(0, units // unroll, body, 0)

    win = x_ref.shape[1] // 2
    lines = QB // win
    copies = []
    for slab in range(slabs):
        own = lax.axis_index("tile") // (2 * TILE_COLS)
        place = pl.ds(pl.multiple_of((own ^ steps[slab]) * lines, lines), lines)
        for w in range(2):
            cols = slice(w * win, w * win + win)
            y = lax.dot_general(
                ot[slab, w], wp_ref[...], (((0,), (0,)), ((), ())), preferred_element_type=F32
            )
            y = y.reshape(2, 4, lines // 2, win // 4, dim).transpose(0, 2, 1, 3, 4).reshape(lines, win, dim)
            y = x_ref[place, cols, :].astype(F32) + y + bp_ref[...].reshape(1, dim)
            stage[slab, :, cols, :] = y.astype(BF)
        copy = pltpu.make_async_copy(stage.at[slab], out_ref.at[place], sems.at[slab])
        copy.start()
        copies.append(copy)
    for copy in copies:
        copy.wait()


def attention(steps, queries, keys, values, tile_map, wp, bp, started=None):
    rows, cols, dim = tile_map.shape
    slabs = len(queries)
    lines = QB * 2 // cols
    more = [] if started is None else [started]
    anywhere = pl.BlockSpec(memory_space=pl.ANY)
    return pl.pallas_call(
        functools.partial(attention_kernel, steps),
        in_specs=[VM] * (slabs + 7) + [anywhere] * len(more),
        out_specs=anywhere,
        out_shape=jax.ShapeDtypeStruct(tile_map.shape, BF),
        input_output_aliases={slabs + 7: 0} if more else {},
        scratch_shapes=[
            pltpu.VMEM((slabs, HEADS, QB, 128), BF),
            pltpu.VMEM((2, 2, rows * cols // 2, QB), F32),
            pltpu.VMEM((2, 2, 8, QB), F32),
            pltpu.VMEM((slabs, 2, dim, QB), BF),
            pltpu.VMEM((slabs, lines, cols, dim), BF),
            pltpu.SemaphoreType.DMA((slabs,)),
        ],
        compiler_params=pltpu.CompilerParams(vmem_limit_bytes=40 * 2**20),
        cost_estimate=pl.CostEstimate(
            flops=8 * slabs * QB * 1024 * dim * 8,
            bytes_accessed=12 * 2**20,
            transcendentals=48 * slabs * QB * 1024,
        ),
        name="attention",
    )(*queries, *keys, *values, tile_map, wp, bp, *more)


def whole(array):
    return pl.BlockSpec(array.shape, lambda *i: (0,) * len(array.shape), pipeline_mode=pl.Buffered(1))


def wholes(*arrays):
    return [whole(array) for array in arrays]


def at_level(array, level):
    shape = (None,) + array.shape[1:]
    return pl.BlockSpec(shape, lambda *i: (level,) + (0,) * (len(shape) - 1), pipeline_mode=pl.Buffered(1))


def position():
    index = lax.axis_index("tile")
    return index // TILE_COLS, index % TILE_COLS


def params(mib):
    return pltpu.CompilerParams(vmem_limit_bytes=mib * 2**20)


def cost(flops, size):
    return pl.CostEstimate(flops=flops, bytes_accessed=size, transcendentals=0)


def round_up(count, unit):
    return -(-count // unit) * unit


def odd_column():
    return position()[1] % 2 == 1


def give_sides(keep_r, keep_l, to_partner, to_cross):
    odd = odd_column()
    to_partner[...] = jnp.where(odd, keep_l[...], keep_r[...]).astype(BF)
    to_cross[...] = jnp.where(odd, keep_r[...], keep_l[...]).astype(BF)


def take_sides(partner_ref, cross_ref):
    odd = odd_column()
    partner, cross = partner_ref[...].astype(F32), cross_ref[...].astype(F32)
    return jnp.where(odd, partner, cross), jnp.where(odd, cross, partner)


def side_pieces_kernel(before, after, left_ref, right_ref, to_partner, to_cross, keep_r, keep_l):
    high = left_ref.shape[0]
    span = right_ref.shape[1]
    keep_l[...] = jnp.zeros_like(keep_l)
    for r in range(high):
        keep_r[r * before : r * before + before, :] = right_ref[r].astype(F32)[span - before :]
        keep_l[r * before : r * before + after, :] = left_ref[r].astype(F32)[:after]
    give_sides(keep_r, keep_l, to_partner, to_cross)


def side_pieces(tile, before, after):
    high, wide, dim = tile.shape
    return pl.pallas_call(
        functools.partial(side_pieces_kernel, before, after),
        grid=(1,),
        in_specs=[
            pl.BlockSpec((high, 16, dim), lambda i: (0, 0, 0)),
            pl.BlockSpec((high, 16, dim), lambda i: (0, wide // 16 - 1, 0)),
        ],
        out_shape=[jax.ShapeDtypeStruct((high * before, dim), BF)] * 2,
        scratch_shapes=[pltpu.VMEM((high * before, dim), F32)] * 2,
        compiler_params=params(12),
        cost_estimate=cost(0, 2 * 2**20),
        name="side_pieces",
    )(tile, tile)


def line_pieces_kernel(before, after, high, top_ref, low_ref, left_ref, right_ref, to_low, to_up, keep_d, keep_u, side_l, side_r):
    wide = top_ref.shape[1]
    full = before + wide + after
    side_l[...], side_r[...] = take_sides(left_ref, right_ref)
    keep_d[...] = jnp.zeros_like(keep_d)
    keep_u[...] = jnp.zeros_like(keep_u)

    def fill(keep, line, r, values):
        base = line * full
        keep[base : base + before, :] = side_l[r * before : r * before + before, :]
        keep[base + before : base + before + wide, :] = values
        keep[base + before + wide : base + full, :] = side_r[r * before : r * before + after, :]

    for line in range(before):
        fill(keep_d, line, high - before + line, low_ref[line].astype(F32))
    for line in range(after):
        fill(keep_u, line, line, top_ref[line].astype(F32))
    to_low[...] = keep_d[...].astype(BF)
    to_up[...] = keep_u[...].astype(BF)


def line_pieces(tile, left, right, before, after):
    high, wide, dim = tile.shape
    full = before + wide + after
    down = round_up(before * full, 16)
    up = round_up(after * full, 16)
    low_size = before if high % before == 0 else 8
    assert high % low_size == 0
    return pl.pallas_call(
        functools.partial(line_low_kernel, low_size, before, after, high),
        grid=(1,),
        in_specs=[
            pl.BlockSpec((after if high % after == 0 else 8, wide, dim), lambda i: (0, 0, 0)),
            pl.BlockSpec((low_size, wide, dim), lambda i: (high // low_size - 1, 0, 0)),
            whole(left),
            whole(right),
        ],
        out_shape=[jax.ShapeDtypeStruct((down, dim), BF), jax.ShapeDtypeStruct((up, dim), BF)],
        scratch_shapes=[
            pltpu.VMEM((down, dim), F32),
            pltpu.VMEM((up, dim), F32),
            pltpu.VMEM(left.shape, F32),
            pltpu.VMEM(right.shape, F32),
        ],
        compiler_params=params(12),
        cost_estimate=cost(0, 2**20),
        name="line_pieces",
    )(tile, tile, left, right)


def line_low_kernel(low_size, before, after, high, top_ref, low_ref, *rest):
    line_pieces_kernel(before, after, high, top_ref, low_ref.at[pl.ds(low_size - before, before)], *rest)


def moved_by(value, rows, cols):
    count = lax.axis_size("tile")
    pairs = []
    for t in range(count):
        r, c = t // TILE_COLS + rows, t % TILE_COLS + cols
        if 0 <= r < count // TILE_COLS and 0 <= c < TILE_COLS:
            pairs.append((t, r * TILE_COLS + c))
    return lax.ppermute(value, "tile", pairs)


def after_these(value, *others):
    return lax.optimization_barrier((value,) + others)[0]


def exchange_rims(tile, pieces, before, after, early, beside):
    tiles = range(lax.axis_size("tile"))
    left = lax.ppermute(pieces[0], "tile", [(t, t ^ 1) for t in tiles])
    between = [(t, t + 1) for t in tiles if t % 2 == 1 and (t + 1) % TILE_COLS]
    right = lax.ppermute(pieces[1], "tile", between + [(b, a) for a, b in between])
    left, right, *first = lax.optimization_barrier((left, right, *early(pieces[0])))
    down, up = line_pieces(tile, left, right, before, after)
    above, below = moved_by(down, 1, 0), moved_by(up, -1, 0)
    result = beside((left, right), down)
    above, below, *result = lax.optimization_barrier((above, below, *result))
    return (left, right, above, below), first, result


def erf_gelu(y):
    return 0.5 * y * (1.0 + lax.erf(y * 0.7071067811865476))


def conv_gelu(padded, kernel_ref, g_ref, own_rows, own_cols, part_ref):
    rows, cols, dim = g_ref.shape
    column = lax.broadcasted_iota(jnp.int32, (cols, 128), 0)
    mine = (column >= own_cols[0]) & (column < own_cols[1])
    for group in range(dim // 128):
        lanes = slice(128 * group, 128 * group + 128)
        taps = [[kernel_ref[a, b : b + 1, lanes].astype(F32) for b in range(3)] for a in range(3)]

        def line(r, total):
            y = None
            for a in range(3):
                for b in range(3):
                    term = padded[r + a, b : b + cols, lanes] * taps[a][b]
                    y = term if y is None else y + term
            g = erf_gelu(y)
            g_ref[r, :, lanes] = g
            counted = jnp.sum(jnp.where(mine, g, 0.0).reshape(cols // 8, 8, 128), axis=0)
            return total + jnp.where((r >= own_rows[0]) & (r < own_rows[1]), counted, 0.0)

        total = lax.fori_loop(0, rows, line, jnp.zeros((8, 128), F32), unroll=True)
        total = jnp.sum(total, axis=0, keepdims=True)
        part_ref[:, group, :] += jnp.broadcast_to(total, (part_ref.shape[0], 128))


def copy_centre(padded, rest_ref):
    rows, cols, _ = rest_ref.shape

    def line(r, _):
        rest_ref[r] = padded[r + 1, 1 : 1 + cols, :].astype(BF)
        return 0

    lax.fori_loop(0, rows, line, 0)


def thirds(row):
    high = row.astype(BF).astype(F32)
    mid = (row - high).astype(BF).astype(F32)
    low = row - high - mid
    index = lax.broadcasted_iota(jnp.int32, (16, row.shape[1]), 0)
    block = jnp.where(index == 0, high, jnp.where(index == 1, mid, jnp.where(index == 2, low, 0.0)))
    return block.astype(BF)


def gate_row(sums_ref, cells, reduce_ref, expand_ref):
    total = jnp.sum(sums_ref[...], axis=0)
    groups = reduce_ref.shape[1] // 128
    mean = jnp.concatenate([total[group : group + 1] for group in range(groups)], axis=1) / cells
    inner = lax.dot_general(
        thirds(mean), reduce_ref[...], (((1,), (1,)), ((), ())), preferred_element_type=F32
    )
    inner = jnp.sum(inner, axis=0, keepdims=True)
    inner = erf_gelu(inner)
    outer = jnp.sum(jnp.dot(thirds(inner), expand_ref[...], preferred_element_type=F32), axis=0, keepdims=True)
    return 1.0 / (1.0 + jnp.exp(-outer))


def mix_lines(g_ref, gate, mix_ref, rest_ref, z_ref, lines, bounds):
    rows, cols, dim = g_ref.shape
    row_low, row_high, col_low, col_high = bounds
    column = lax.broadcasted_iota(jnp.int32, (cols, 1), 0)
    inside = (column >= col_low) & (column < col_high)
    u = (g_ref[...] * gate).astype(BF).reshape(rows * cols, dim)
    product = jnp.dot(u, mix_ref[...], preferred_element_type=F32).reshape(rows, cols, dim)
    for k in range(rows):
        z = (rest_ref[k].astype(F32) + product[k]).astype(BF).astype(F32)
        keep = inside & (lines[k] >= row_low) & (lines[k] < row_high)
        z_ref[lines[k]] = jnp.where(keep, z, -jnp.inf)


def pooled_line(z_ref, line_ref, i, count):
    most = jnp.maximum(jnp.maximum(z_ref[2 * i], z_ref[2 * i + 1]), z_ref[2 * i + 2])
    groups = []
    for group in range(line_ref.shape[0]):
        line_ref[group] = most[:, 128 * group : 128 * group + 128]
        parts = [line_ref[group, pl.ds(s, count, stride=2), :] for s in range(3)]
        groups.append(jnp.maximum(jnp.maximum(parts[0], parts[1]), parts[2]))
    return jnp.concatenate(groups, axis=1)


def fill_sides(x_ref, left_ref, right_ref, before, after, padded, stage):
    high, wide, _ = x_ref.shape
    full = before + wide + after

    def line(r, _):
        padded[r, before : before + wide, :] = x_ref[r].astype(F32)
        return 0

    lax.fori_loop(0, high, line, 0)
    left, right = take_sides(left_ref, right_ref)
    stage[...] = left
    for r in range(high):
        padded[r, 0:before, :] = stage[r * before : r * before + before, :]
    stage[...] = right
    for r in range(high):
        padded[r, before + wide : full, :] = stage[r * before : r * before + after, :]


def inner_kernel(before, after, x_ref, l_ref, r_ref, kernel_ref, g_ref, rest_ref, part_ref, padded, stage):
    _, wide, _ = x_ref.shape
    step = g_ref.shape[0]
    turn = pl.program_id(0)

    @pl.when(turn == 0)
    def _():
        fill_sides(x_ref, l_ref, r_ref, before, after, padded, stage)
        part_ref[...] = jnp.zeros_like(part_ref)

    block = padded.at[pl.ds(turn * step, step + 2)]
    copy_centre(block, rest_ref)
    conv_gelu(block, kernel_ref, g_ref, (0, step), (before - 1, before - 1 + wide), part_ref)


def activate_inner(tile, left, right, kernels, level, before, after, step):
    high, wide, dim = tile.shape
    rows, cols = high - 2, round_up(wide + before + after - 2, 8)
    copies = lax.axis_size("tile")
    block = pl.BlockSpec((step, cols, dim), lambda i: (i, 0, 0))
    return pl.pallas_call(
        functools.partial(inner_kernel, before, after),
        grid=(rows // step,),
        in_specs=wholes(tile, left, right) + [at_level(kernels, level)],
        out_specs=[block, block, pl.BlockSpec((copies, 8, 128), lambda i: (0, 0, 0))],
        out_shape=[
            jax.ShapeDtypeStruct((rows, cols, dim), F32),
            jax.ShapeDtypeStruct((rows, cols, dim), BF),
            jax.ShapeDtypeStruct((copies, 8, 128), F32),
        ],
        scratch_shapes=[
            pltpu.VMEM((high, round_up(cols + 2, 8), dim), F32),
            pltpu.VMEM((max(left.shape[0], right.shape[0]), dim), F32),
        ],
        compiler_params=params(28 if level == 0 else 20),
        cost_estimate=cost(400 * rows * cols * dim, 6 * rows * cols * dim),
        name="activate_inner",
    )(tile, left, right, kernels)


def edge_kernel(high, before, after, top_ref, low_ref, l_ref, r_ref, a_ref, b_ref, kernel_ref, sum_ref, g_ref, rest_ref, part_ref, upper, lower, side_l, side_r, stage):
    wide = top_ref.shape[1]
    full = before + wide + after
    own = (before - 1, before - 1 + wide)
    side_l[...], side_r[...] = take_sides(l_ref, r_ref)

    def fill(padded, at, r, values):
        padded[at, 0:before, :] = side_l[r * before : r * before + before, :]
        padded[at, before : before + wide, :] = values.astype(F32)
        padded[at, before + wide : full, :] = side_r[r * before : r * before + after, :]

    for k in range(2):
        fill(upper, before + k, k, top_ref[k])
        fill(lower, k, high - 2 + k, low_ref[k])
    stage[: a_ref.shape[0], :] = a_ref[...].astype(F32)
    for k in range(before):
        upper[k, 0:full, :] = stage[k * full : k * full + full, :]
    stage[: b_ref.shape[0], :] = b_ref[...].astype(F32)
    for k in range(after):
        lower[2 + k, 0:full, :] = stage[k * full : k * full + full, :]
    part_ref[...] = sum_ref[...]
    up, low = pl.ds(0, before), pl.ds(before, after)
    copy_centre(upper, rest_ref.at[up])
    copy_centre(lower, rest_ref.at[low])
    conv_gelu(upper, kernel_ref, g_ref.at[up], (before - 1, before), own, part_ref)
    conv_gelu(lower, kernel_ref, g_ref.at[low], (0, 1), own, part_ref)


def activate_edge(tile, rims, kernels, part, level, before, after):
    high, wide, dim = tile.shape
    cols = round_up(wide + before + after - 2, 8)
    padded = round_up(cols + 2, 8)
    stage = max(r.shape[0] for r in rims)
    left, right, above, below = rims
    lines = before + after
    outs = [
        jax.ShapeDtypeStruct((lines, cols, dim), F32),
        jax.ShapeDtypeStruct((lines, cols, dim), BF),
        jax.ShapeDtypeStruct(part.shape, F32),
    ]
    return pl.pallas_call(
        functools.partial(edge_kernel, high, before, after),
        grid=(1,),
        in_specs=[
            pl.BlockSpec((2, wide, dim), lambda i: (0, 0, 0)),
            pl.BlockSpec((2, wide, dim), lambda i: (high // 2 - 1, 0, 0)),
        ]
        + wholes(*rims)
        + [at_level(kernels, level), whole(part)],
        out_specs=wholes(*outs),
        out_shape=outs,
        scratch_shapes=[
            pltpu.VMEM((before + 2, padded, dim), F32),
            pltpu.VMEM((after + 2, padded, dim), F32),
            pltpu.VMEM(left.shape, F32),
            pltpu.VMEM(right.shape, F32),
            pltpu.VMEM((stage, dim), F32),
        ],
        compiler_params=params(16),
        cost_estimate=cost(400 * lines * cols * dim, 6 * lines * cols * dim),
        name="activate_edge",
    )(tile, tile, *rims, kernels, part)


def mix0_kernel(cells, before, after, sums, red, exp, mix, g_ref, rest, g_edge, rest_edge, x_out, to_partner, to_cross, gates, z, line, keep_r, keep_l):
    step, cols, dim = g_ref.shape
    high, wide, _ = x_out.shape
    turn = pl.program_id(0)

    pos = position()
    bounds = (jnp.where(pos[0] == 0, 1, 0), z.shape[0], jnp.where(pos[1] == 0, 1, 0), cols)

    @pl.when(turn == 0)
    def _():
        gates[...] = jnp.broadcast_to(gate_row(sums, cells, red, exp), gates.shape)
        keep_l[...] = jnp.zeros_like(keep_l)
        mix_lines(g_edge, gates[:1, :], mix, rest_edge, z, (0, 1, z.shape[0] - 1), bounds)

    mix_lines(g_ref, gates[:1, :], mix, rest, z, [2 + turn * step + k for k in range(step)], bounds)

    @pl.when(turn == pl.num_programs(0) - 1)
    def _():
        for i in range(high):
            out = pooled_line(z, line, i, wide)
            x_out[i] = out.astype(BF)
            keep_r[i * before : i * before + before, :] = out[wide - before :]
            keep_l[i * before : i * before + after, :] = out[:after]
        give_sides(keep_r, keep_l, to_partner, to_cross)


def level_specs(sums, red, exp, mix, level):
    return [whole(sums), at_level(red, level), at_level(exp, level), at_level(mix, level)]


def mix0(sums, red, exp, mix, g, rest, edges, cells, high, wide, before, after, step):
    rows, cols, dim = g.shape
    block = pl.BlockSpec((step, cols, dim), lambda i: (i, 0, 0))
    outs = [
        jax.ShapeDtypeStruct((high, wide, dim), BF),
        jax.ShapeDtypeStruct((high * before, dim), BF),
        jax.ShapeDtypeStruct((high * before, dim), BF),
    ]
    return pl.pallas_call(
        functools.partial(mix0_kernel, cells, before, after),
        grid=(rows // step,),
        in_specs=level_specs(sums, red, exp, mix, 0) + [block, block] + wholes(*edges),
        out_specs=wholes(*outs),
        out_shape=outs,
        scratch_shapes=[
            pltpu.VMEM((8, dim), F32),
            pltpu.VMEM((rows + 3, cols, dim), F32),
            pltpu.VMEM((dim // 128, cols, 128), F32),
            pltpu.VMEM((high * before, dim), F32),
            pltpu.VMEM((high * before, dim), F32),
        ],
        compiler_params=params(32),
        cost_estimate=cost(2 * rows * cols * dim * dim, 6 * rows * cols * dim),
        name="mix0",
    )(sums, red, exp, mix, g, rest, *edges)


def mix1_kernel(cells, size, before, sums, red, exp, mix, g_ref, rest, g_edge, rest_edge, kernel, g_out, rest_out, part, z, line, padded):
    rows, cols, dim = g_ref.shape
    side_r, side_c, map_side = size
    gate = gate_row(sums, cells, red, exp)
    shift = before - 1
    pos = position()
    row_low = shift - pos[0] * side_r
    col_low = shift - pos[1] * side_c
    bounds = (row_low, row_low + map_side, col_low, col_low + map_side)
    inner = range(before, before + rows)
    mix_lines(g_ref, gate, mix, rest, z, inner, bounds)
    mix_lines(g_edge, gate, mix, rest_edge, z, [k for k in range(z.shape[0]) if k not in inner], bounds)
    count_r, count_c = padded.shape[0], (cols - 1) // 2
    row_two = 2 - pos[0] * (side_r // 2)
    col_two = 2 - pos[1] * (side_c // 2)
    column = lax.broadcasted_iota(jnp.int32, (count_c, 1), 0)
    inside = (column >= col_two) & (column < col_two + map_side // 2)
    for i in range(count_r):
        out = pooled_line(z, line, i, count_c)
        keep = inside & (i >= row_two) & (i < row_two + map_side // 2)
        padded[i, 0:count_c, :] = jnp.where(keep, out, 0.0)
    copy_centre(padded, rest_out)
    part[...] = jnp.zeros_like(part)
    conv_gelu(padded, kernel, g_out, (1, 1 + side_r // 2), (1, 1 + side_c // 2), part)


def mix1(sums, red, exp, mix, g, rest, edges, kernels, cells, size, before):
    rows, cols, dim = g.shape
    rows += edges[0].shape[0]
    out_rows, out_cols = (rows - 1) // 2 - 2, round_up((cols - 1) // 2 - 2, 8)
    outs = [
        jax.ShapeDtypeStruct((out_rows, out_cols, dim), F32),
        jax.ShapeDtypeStruct((out_rows, out_cols, dim), BF),
        jax.ShapeDtypeStruct(sums.shape, F32),
    ]
    return pl.pallas_call(
        functools.partial(mix1_kernel, cells, size, before),
        grid=(1,),
        in_specs=level_specs(sums, red, exp, mix, 1) + wholes(g, rest, *edges) + [at_level(kernels, 2)],
        out_specs=wholes(*outs),
        out_shape=outs,
        scratch_shapes=[
            pltpu.VMEM((rows, cols, dim), F32),
            pltpu.VMEM((dim // 128, cols, 128), F32),
            pltpu.VMEM((out_rows + 2, round_up(out_cols + 2, 8), dim), F32),
        ],
        compiler_params=params(18),
        cost_estimate=cost(2 * rows * cols * dim * dim, 6 * rows * cols * dim),
        name="mix1",
    )(sums, red, exp, mix, g, rest, *edges, kernels)


def mix2_kernel(cells, high, wide, sums, red, exp, mix, g_ref, rest, x_out, z, line, keep):
    rows, cols, dim = g_ref.shape
    gate = gate_row(sums, cells, red, exp)
    pos = position()
    bounds = (jnp.where(pos[0] == 0, 1, 0), rows, jnp.where(pos[1] == 0, 1, 0), cols)
    mix_lines(g_ref, gate, mix, rest, z, range(rows), bounds)
    for i in range(high):
        keep[i * wide : i * wide + wide, :] = pooled_line(z, line, i, wide)
    x_out[...] = jnp.broadcast_to(keep[...].astype(BF), x_out.shape)


def mix2(sums, red, exp, mix, g, rest, cells, high, wide, copies):
    rows, cols, dim = g.shape
    out = jax.ShapeDtypeStruct((copies, high * wide, dim), BF)
    return pl.pallas_call(
        functools.partial(mix2_kernel, cells, high, wide),
        grid=(1,),
        in_specs=level_specs(sums, red, exp, mix, 2) + wholes(g, rest),
        out_specs=whole(out),
        out_shape=out,
        scratch_shapes=[
            pltpu.VMEM((rows, cols, dim), F32),
            pltpu.VMEM((dim // 128, cols, 128), F32),
            pltpu.VMEM((high * wide, dim), F32),
        ],
        compiler_params=params(10),
        cost_estimate=cost(2 * rows * cols * dim * dim, 6 * rows * cols * dim),
        name="mix2",
    )(sums, red, exp, mix, g, rest)


def everyones(copies):
    return lax.all_to_all(copies, "tile", 0, 0, tiled=True)


def query_slab(tile_map, dw_kernel, se_reduce, se_expand, mix_weight, keys_of):
    high, wide, dim = tile_map.shape
    tiles = lax.axis_size("tile")
    cells = high * wide * tiles
    group = 2 * TILE_COLS
    def inner(tile, level, sides, held, *halos):
        return activate_inner(after_these(tile, held), *sides, dw_kernel, level, *halos)

    rims, (kt0, vt0), (g, rest, part) = exchange_rims(
        tile_map,
        side_pieces(tile_map, 2, 1),
        2,
        1,
        lambda held: keys_of(0, held),
        lambda sides, held: inner(tile_map, 0, sides, held, 2, 1, 10),
    )
    *edges, part = activate_edge(tile_map, rims, dw_kernel, part, 0, 2, 1)
    coarse, *sides = mix0(
        everyones(part), se_reduce, se_expand, mix_weight, g, rest, edges, cells, high // 2, wide // 2, 6, 3, 10
    )

    rims, (kt1, vt1), (g, rest, part) = exchange_rims(
        coarse,
        sides,
        6,
        3,
        lambda held: keys_of(1, held),
        lambda sides, held: inner(coarse, 1, sides, held, 6, 3, high // 2 - 2),
    )
    *edges, part = activate_edge(coarse, rims, dw_kernel, part, 1, 6, 3)
    size = (high // 2, wide // 2, high // 2 * (tiles // TILE_COLS))
    g, rest, part = mix1(
        everyones(part), se_reduce, se_expand, mix_weight, g, rest, edges, dw_kernel, cells // 4, size, 6
    )
    query = mix2(
        everyones(part), se_reduce, se_expand, mix_weight, g, rest, cells // 16, high // 8, wide // 8, group
    )
    groups = [list(range(group * x, group * x + group)) for x in range(tiles // group)]
    slab = lax.all_to_all(query, "tile", 0, 0, tiled=True, axis_index_groups=groups)
    return slab.reshape(-1, dim), (kt0, kt1), (vt0, vt1)


def body(
    features,
    dw_kernel,
    se_reduce,
    se_expand,
    mix_weight,
    norm_gain,
    kv_weight,
    kv_bias,
    proj_weight,
    proj_bias,
):
    tile_map = features[0]
    se_reduce = jnp.swapaxes(se_reduce, 1, 2)

    def keys_of(window, held):
        return keys_values(after_these(tile_map, held), norm_gain, kv_weight, kv_bias, window)

    slab, keys, values = query_slab(tile_map, dw_kernel, se_reduce, se_expand, mix_weight, keys_of)
    tiles = lax.axis_size("tile")
    group = 2 * TILE_COLS
    def from_x(value, step):
        return lax.ppermute(value, "tile", [(t, t ^ group * step) for t in range(tiles)])

    near = [from_x(slab, 1), from_x(slab, 3)]
    rest = (keys, values, tile_map, proj_weight, proj_bias)
    out = attention((0,), [slab], *rest)
    far, out = lax.optimization_barrier((slab, out))
    far = from_x(far, 2)
    out = attention((1, 3), near, *rest, out)
    return attention((2,), [far], *rest, out)[None]


def solution(mesh):
    in_specs = (P(("scene", "tile"), None, None, None), P(), P(), P(), P(), P(), P(), P(), P(), P())
    out_specs = P(("scene", "tile"), None, None, None)
    return jax.shard_map(body, mesh=mesh, in_specs=in_specs, out_specs=out_specs, check_vma=False)
```

profile of v0, /device:TPU:0, one launch (start us, length us, event | category | flops | bytes accessed | tf_op | source)
XLA Modules:
  0.0 176.4 jit_solution(9603405391349774689)
XLA Ops:
  0.0 1.9 %copy-done = bf16[1,32,64,768]{3,2,1,0:T(8,128)(2,1)S(1)} copy-done((bf16[1,32,64,768]{3,2,1,0:T(8,128)(2,1)S(1)}, bf16[1,32,64,768]{3,2,1,0:T(8,128)(2,1)}, u32[]{:S(2)}) %copy-start) | copy-done | bytes 3145752
  1.9 0.2 side_pieces.1
  2.1 0.8 collective-permute-start.1
  2.9 3.6 %collective-permute-start = (bf16[64,768]{1,0:T(8,128)(2,1)S(1)}, bf16[64,768]{1,0:T(8,128)(2,1)S(1)}, u32[]{:S(2)}, u32[]{:S(2)}) collective-permute-start(bf16[64,768]{1,0:T(8,128)(2,1)S(1)} %get-tuple-element.57), channel_id=1, source_target_pairs={{0,1},{1,0},{2,3},{3,2},{4,5},{5,4},{6,7},{7,6},{8,9},{9,8},{10,11... | collective-permute-start | bytes 294920 | tf_op jit(solution)/shard_map/ppermute | solution.py:320
  6.5 4.7 %keys_values.2 = (bf16[6,1024,128]{2,1,0:T(8,128)(2,1)S(1)}, bf16[768,1024]{1,0:T(8,128)(2,1)S(1)}) custom-call(bf16[32,64,768]{2,1,0:T(8,128)(2,1)S(1)} %bitcast.6, f32[768]{0:T(1024)S(1)} %copy-done.9, bf16[768,1536]{1,0:T(8,128)(2,1)S(1)} %copy-done.6, f32[1536]{0:T(1024)S(1)} %copy-done.8), custom_call_target="tpu_custom_call" | custom-call | flops 4831838208 | bytes 8388608 | tf_op jit(solution)/shard_map/keys_values/pallas_call | solution.py:41
  11.2 0.1 line_pieces.2
  11.4 5.5 %collective-permute-start.2 = (bf16[144,768]{1,0:T(8,128)(2,1)S(1)}, bf16[144,768]{1,0:T(8,128)(2,1)S(1)}, u32[]{:S(2)}, u32[]{:S(2)}) collective-permute-start(bf16[144,768]{1,0:T(8,128)(2,1)S(1)} %get-tuple-element.64), channel_id=1, source_target_pairs={{0,4},{1,5},{2,6},{3,7},{4,8},{5,9},{6,10},{7,11},{8,12},{9,13},{1... | collective-permute-start | bytes 663560 | tf_op jit(solution)/shard_map/ppermute | solution.py:311
  16.9 1.3 collective-permute-start.3
  18.2 10.4 %activate_inner.2 = (f32[30,72,768]{2,1,0:T(8,128)S(1)}, bf16[30,72,768]{2,1,0:T(8,128)(2,1)S(1)}, f32[32,8,128]{2,1,0:T(8,128)S(1)}) custom-call(bf16[32,64,768]{2,1,0:T(8,128)(2,1)S(1)} %bitcast.9, bf16[64,768]{1,0:T(8,128)(2,1)S(1)} %collective-permute-done.rest_0_.l_ref, bf16[64,768]{1,0:T(8,128)(2,1)S(1)} %collective-permute-done.1.rest_1_.r_ref, ...), custom_call_target="tpu_custom_call" | custom-call | flops 663552000 | bytes 9953280 | tf_op jit(solution)/shard_map/activate_inner/pallas_call | solution.py:452
  28.6 1.3 activate_edge.2
  29.9 16.1 %all_to_all.20.sums = f32[32,8,128]{2,1,0:T(8,128)S(1)} all-to-all(f32[32,8,128]{2,1,0:T(8,128)S(1)} %get-tuple-element.73), channel_id=1, replica_groups=mesh['scene'=4,'tile'=32] {'tile'}, dimensions={0} | all-to-all | bytes 262144 | tf_op jit(solution)/shard_map/all_to_all | solution.py:677
  46.0 5.3 %mix0.1 = (bf16[16,32,768]{2,1,0:T(8,128)(2,1)S(1)}, bf16[96,768]{1,0:T(8,128)(2,1)S(1)}, bf16[96,768]{1,0:T(8,128)(2,1)S(1)}) custom-call(f32[32,8,128]{2,1,0:T(8,128)S(1)} %all_to_all.20.sums, bf16[3,192,768]{2,1,0:T(8,128)(2,1)S(1)} %bitcast.16, bf16[3,192,768]{2,1,0:T(8,128)(2,1)S(1)} %copy-done.4, bf16[3,768,768]{2,1,0:T(8,128)(2,1)S(1)} %copy-done.2, ...), custom_call_target="tpu_custom_call" | custom-call | flops 2548039680 | bytes 9953280 | tf_op jit(solution)/shard_map/mix0/pallas_call | solution.py:574
  51.3 0.2 collective-permute-start.4
  51.5 0.7 collective-permute-start.5
  52.2 4.7 %keys_values.3 = (bf16[6,1024,128]{2,1,0:T(8,128)(2,1)S(1)}, bf16[768,1024]{1,0:T(8,128)(2,1)S(1)}) custom-call(bf16[32,64,768]{2,1,0:T(8,128)(2,1)S(1)} %bitcast.12, f32[768]{0:T(1024)S(1)} %copy-done.9, bf16[768,1536]{1,0:T(8,128)(2,1)S(1)} %copy-done.6, f32[1536]{0:T(1024)S(1)} %copy-done.8), custom_call_target="tpu_custom_call" | custom-call | flops 4831838208 | bytes 8388608 | tf_op jit(solution)/shard_map/keys_values/pallas_call | solution.py:41
  56.9 0.2 line_pieces.3
  57.2 2.9 %collective-permute-start.6 = (bf16[256,768]{1,0:T(8,128)(2,1)S(1)}, bf16[256,768]{1,0:T(8,128)(2,1)S(1)}, u32[]{:S(2)}, u32[]{:S(2)}) collective-permute-start(bf16[256,768]{1,0:T(8,128)(2,1)S(1)} %get-tuple-element.86), channel_id=1, source_target_pairs={{0,4},{1,5},{2,6},{3,7},{4,8},{5,9},{6,10},{7,11},{8,12},{9,13},{1... | collective-permute-start | bytes 1179656 | tf_op jit(solution)/shard_map/ppermute | solution.py:311
  60.1 1.5 collective-permute-start.7
  61.6 3.0 %activate_inner.3 = (f32[14,40,768]{2,1,0:T(8,128)S(1)}, bf16[14,40,768]{2,1,0:T(8,128)(2,1)S(1)}, f32[32,8,128]{2,1,0:T(8,128)S(1)}) custom-call(bf16[16,32,768]{2,1,0:T(8,128)(2,1)S(1)} %get-tuple-element.88.top_ref.low_ref.x_ref, bf16[96,768]{1,0:T(8,128)(2,1)S(1)} %collective-permute-done.4.rest_0_.l_ref, ...), custom_call_target="tpu_custom_call" | custom-call | flops 172032000 | bytes 2580480 | tf_op jit(solution)/shard_map/activate_inner/pallas_call | solution.py:452
  64.6 4.8 %collective-permute-done.7.b_ref = bf16[128,768]{1,0:T(8,128)(2,1)S(1)} collective-permute-done((bf16[128,768]{1,0:T(8,128)(2,1)S(1)}, bf16[128,768]{1,0:T(8,128)(2,1)S(1)}, u32[]{:S(2)}, u32[]{:S(2)}) %collective-permute-start.7) | collective-permute-done | bytes 196640 | tf_op jit(solution)/shard_map/ppermute | solution.py:311
  69.4 2.1 %collective-permute-done.6.a_ref = bf16[256,768]{1,0:T(8,128)(2,1)S(1)} collective-permute-done((bf16[256,768]{1,0:T(8,128)(2,1)S(1)}, bf16[256,768]{1,0:T(8,128)(2,1)S(1)}, u32[]{:S(2)}, u32[]{:S(2)}) %collective-permute-start.6) | collective-permute-done | bytes 393248 | tf_op jit(solution)/shard_map/ppermute | solution.py:311
  71.5 2.0 %activate_edge.3 = (f32[9,40,768]{2,1,0:T(8,128)S(1)}, bf16[9,40,768]{2,1,0:T(8,128)(2,1)S(1)}, f32[32,8,128]{2,1,0:T(8,128)S(1)}) custom-call(bf16[16,32,768]{2,1,0:T(8,128)(2,1)S(1)} %get-tuple-element.88.top_ref.low_ref.x_ref, bf16[16,32,768]{2,1,0:T(8,128)(2,1)S(1)} %get-tuple-element.88.top_ref.low_ref.x_ref, ...), custom_call_target="tpu_custom_call" | custom-call | flops 110592000 | bytes 1658880 | tf_op jit(solution)/shard_map/activate_edge/pallas_call | solution.py:512
  73.5 16.7 %all_to_all.21.sums = f32[32,8,128]{2,1,0:T(8,128)S(1)} all-to-all(f32[32,8,128]{2,1,0:T(8,128)S(1)} %get-tuple-element.95), channel_id=1, replica_groups=mesh['scene'=4,'tile'=32] {'tile'}, dimensions={0} | all-to-all | bytes 262144 | tf_op jit(solution)/shard_map/all_to_all | solution.py:677
  90.2 3.2 %mix1.1 = (f32[9,24,768]{2,1,0:T(8,128)S(1)}, bf16[9,24,768]{2,1,0:T(8,128)(2,1)S(1)}, f32[32,8,128]{2,1,0:T(8,128)S(1)}) custom-call(f32[32,8,128]{2,1,0:T(8,128)S(1)} %all_to_all.21.sums, bf16[3,192,768]{2,1,0:T(8,128)(2,1)S(1)} %bitcast.17, bf16[3,192,768]{2,1,0:T(8,128)(2,1)S(1)} %copy-done.4, bf16[3,768,768]{2,1,0:T(8,128)(2,1)S(1)} %copy-done.2, ...), custom_call_target="tpu_custom_call" | custom-call | flops 1085276160 | bytes 4239360 | tf_op jit(solution)/shard_map/mix1/pallas_call | solution.py:628
  93.4 11.3 %all_to_all.22.sums = f32[32,8,128]{2,1,0:T(8,128)S(1)} all-to-all(f32[32,8,128]{2,1,0:T(8,128)S(1)} %get-tuple-element.100), channel_id=1, replica_groups=mesh['scene'=4,'tile'=32] {'tile'}, dimensions={0} | all-to-all | bytes 262144 | tf_op jit(solution)/shard_map/all_to_all | solution.py:677
  104.7 0.9 mix2.1
  105.6 11.3 %all_to_all.23 = bf16[8,32,768]{2,1,0:T(8,128)(2,1)S(1)} all-to-all(bf16[8,32,768]{2,1,0:T(8,128)(2,1)S(1)} %mix2.1), channel_id=1, replica_groups={{0,1,2,3,4,5,6,7},{8,9,10,11,12,13,14,15},{16,17,18,19,20,21,22,23},{24..., dimensions={0} | all-to-all | bytes 786432 | tf_op jit(solution)/shard_map/all_to_all | solution.py:718
  116.9 1.1 collective-permute-start.10
  118.1 14.3 %attention.3.refs_9_ = bf16[32,64,768]{2,1,0:T(8,128)(2,1)} custom-call(bf16[256,768]{1,0:T(8,128)(2,1)S(1)} %bitcast.21, bf16[6,1024,128]{2,1,0:T(8,128)(2,1)S(1)} %get-tuple-element.103.refs_1_.refs_2_, bf16[6,1024,128]{2,1,0:T(8,128)(2,1)S(1)} %get-tuple-element.104.refs_2_.refs_3_, bf16[768,1024]{1,0:T(8,128)(2,1)S(1)} %get-tuple-element.105.refs_3_.refs_4_, ...), custom_call_target="tpu_custom_call" | custom-call | flops 12884901888 | bytes 12582912 | tf_op jit(solution)/shard_map/attention/pallas_call | solution.py:153
  132.4 3.5 %collective-permute-start.8 = (bf16[256,768]{1,0:T(8,128)(2,1)S(1)}, bf16[256,768]{1,0:T(8,128)(2,1)S(1)}, u32[]{:S(2)}, u32[]{:S(2)}) collective-permute-start(bf16[256,768]{1,0:T(8,128)(2,1)S(1)} %bitcast.22), channel_id=1, source_target_pairs={{0,16},{1,17},{2,18},{3,19},{4,20},{5,21},{6,22},{7,23},{8,24},{9,... | collective-permute-start | bytes 1179656 | tf_op jit(solution)/shard_map/ppermute | solution.py:744
  136.0 26.0 %attention.4.refs_8_ = bf16[32,64,768]{2,1,0:T(8,128)(2,1)} custom-call(bf16[256,768]{1,0:T(8,128)(2,1)S(1)} %collective-permute-done.9.refs_0_, bf16[256,768]{1,0:T(8,128)(2,1)S(1)} %collective-permute-done.10.refs_1_, bf16[6,1024,128]{2,1,0:T(8,128)(2,1)S(1)} %get-tuple-element.103.refs_1_.refs_2_, ...), custom_call_target="tpu_custom_call", output_to_operand_aliasing={{}: (9, {})} | custom-call | flops 25769803776 | bytes 12582912 | tf_op jit(solution)/shard_map/attention/pallas_call | solution.py:153
  162.0 14.3 %attention.5 = bf16[32,64,768]{2,1,0:T(8,128)(2,1)} custom-call(bf16[256,768]{1,0:T(8,128)(2,1)S(1)} %collective-permute-done.8.refs_0_, bf16[6,1024,128]{2,1,0:T(8,128)(2,1)S(1)} %get-tuple-element.103.refs_1_.refs_2_, bf16[6,1024,128]{2,1,0:T(8,128)(2,1)S(1)} %get-tuple-element.104.refs_2_.refs_3_, ...), custom_call_target="tpu_custom_call", output_to_operand_aliasing={{}: (8, {})} | custom-call | flops 12884901888 | bytes 12582912 | tf_op jit(solution)/shard_map/attention/pallas_call | solution.py:153
  (31 shorter events, 0.2 us)
Async XLA Ops:
  0.0 1.9 %copy-start = (bf16[1,32,64,768]{3,2,1,0:T(8,128)(2,1)S(1)}, bf16[1,32,64,768]{3,2,1,0:T(8,128)(2,1)}, u32[]{:S(2)}) copy-start(bf16[1,32,64,768]{3,2,1,0:T(8,128)(2,1)} %param.10) | copy-start | bytes 9437188
  1.9 4.6 %copy-start.1 = (bf16[1,32,64,768]{3,2,1,0:T(8,128)(2,1)S(1)}, bf16[1,32,64,768]{3,2,1,0:T(8,128)(2,1)}, u32[]{:S(2)}) copy-start(bf16[1,32,64,768]{3,2,1,0:T(8,128)(2,1)} %param.10) | copy-start | bytes 9437188
  1.9 4.6 %copy-start.6 = (bf16[768,1536]{1,0:T(8,128)(2,1)S(1)}, bf16[768,1536]{1,0:T(8,128)(2,1)}, u32[]{:S(2)}) copy-start(bf16[768,1536]{1,0:T(8,128)(2,1)} %w_ref.3) | copy-start | bytes 7077892
  1.9 4.6 %copy-start.8 = (f32[1536]{0:T(1024)S(1)}, f32[1536]{0:T(1024)}, u32[]{:S(2)}) copy-start(f32[1536]{0:T(1024)} %b_ref.3) | copy-start | bytes 18436
  1.9 4.6 %copy-start.9 = (f32[768]{0:T(1024)S(1)}, f32[768]{0:T(1024)}, u32[]{:S(2)}) copy-start(f32[768]{0:T(1024)} %gain_ref.3) | copy-start | bytes 9220
  2.1 9.1 %collective-permute-start.1 = (bf16[64,768]{1,0:T(8,128)(2,1)S(1)}, bf16[64,768]{1,0:T(8,128)(2,1)S(1)}, u32[]{:S(2)}, u32[]{:S(2)}) collective-permute-start(bf16[64,768]{1,0:T(8,128)(2,1)S(1)} %get-tuple-element.58), channel_id=1, source_target_pairs={{1,2},{5,6},{9,10},{13,14},{17,18},{21,22},{25,26},{29,30},{2,1},{... | collective-permute-start | bytes 294920 | tf_op jit(solution)/shard_map/ppermute | solution.py:322
  2.9 8.3 %collective-permute-start = (bf16[64,768]{1,0:T(8,128)(2,1)S(1)}, bf16[64,768]{1,0:T(8,128)(2,1)S(1)}, u32[]{:S(2)}, u32[]{:S(2)}) collective-permute-start(bf16[64,768]{1,0:T(8,128)(2,1)S(1)} %get-tuple-element.57), channel_id=1, source_target_pairs={{0,1},{1,0},{2,3},{3,2},{4,5},{5,4},{6,7},{7,6},{8,9},{9,8},{10,11... | collective-permute-start | bytes 294920 | tf_op jit(solution)/shard_map/ppermute | solution.py:320
  11.2 6.9 %copy-start.5 = (bf16[3,3,3,768]{3,2,1,0:T(4,128)(2,1)S(1)}, bf16[3,3,3,768]{3,2,1,0:T(4,128)(2,1)}, u32[]{:S(2)}) copy-start(bf16[3,3,3,768]{3,2,1,0:T(4,128)(2,1)} %kernel.1) | copy-start | bytes 124420
  11.4 17.2 %collective-permute-start.2 = (bf16[144,768]{1,0:T(8,128)(2,1)S(1)}, bf16[144,768]{1,0:T(8,128)(2,1)S(1)}, u32[]{:S(2)}, u32[]{:S(2)}) collective-permute-start(bf16[144,768]{1,0:T(8,128)(2,1)S(1)} %get-tuple-element.64), channel_id=1, source_target_pairs={{0,4},{1,5},{2,6},{3,7},{4,8},{5,9},{6,10},{7,11},{8,12},{9,13},{1... | collective-permute-start | bytes 663560 | tf_op jit(solution)/shard_map/ppermute | solution.py:311
  16.9 11.7 %collective-permute-start.3 = (bf16[80,768]{1,0:T(8,128)(2,1)S(1)}, bf16[80,768]{1,0:T(8,128)(2,1)S(1)}, u32[]{:S(2)}, u32[]{:S(2)}) collective-permute-start(bf16[80,768]{1,0:T(8,128)(2,1)S(1)} %get-tuple-element.65), channel_id=1, source_target_pairs={{4,0},{5,1},{6,2},{7,3},{8,4},{9,5},{10,6},{11,7},{12,8},{13,9},{1... | collective-permute-start | bytes 368648 | tf_op jit(solution)/shard_map/ppermute | solution.py:311
  28.6 17.4 %copy-start.2 = (bf16[3,768,768]{2,1,0:T(8,128)(2,1)S(1)}, bf16[3,768,768]{2,1,0:T(8,128)(2,1)}, u32[]{:S(2)}) copy-start(bf16[3,768,768]{2,1,0:T(8,128)(2,1)} %mix.5) | copy-start | bytes 10616836
  28.6 17.4 %copy-start.3 = (bf16[3,768,192]{1,2,0:T(8,128)(2,1)S(1)}, bf16[3,768,192]{1,2,0:T(8,128)(2,1)}, u32[]{:S(2)}) copy-start(bf16[3,768,192]{1,2,0:T(8,128)(2,1)} %param.12) | copy-start | bytes 2654212
  28.6 17.4 %copy-start.4 = (bf16[3,192,768]{2,1,0:T(8,128)(2,1)S(1)}, bf16[3,192,768]{2,1,0:T(8,128)(2,1)}, u32[]{:S(2)}) copy-start(bf16[3,192,768]{2,1,0:T(8,128)(2,1)} %exp.5) | copy-start | bytes 2654212
  51.3 5.6 %collective-permute-start.4 = (bf16[96,768]{1,0:T(8,128)(2,1)S(1)}, bf16[96,768]{1,0:T(8,128)(2,1)S(1)}, u32[]{:S(2)}, u32[]{:S(2)}) collective-permute-start(bf16[96,768]{1,0:T(8,128)(2,1)S(1)} %get-tuple-element.79), channel_id=1, source_target_pairs={{0,1},{1,0},{2,3},{3,2},{4,5},{5,4},{6,7},{7,6},{8,9},{9,8},{10,11... | collective-permute-start | bytes 442376 | tf_op jit(solution)/shard_map/ppermute | solution.py:320
  51.5 5.4 %collective-permute-start.5 = (bf16[96,768]{1,0:T(8,128)(2,1)S(1)}, bf16[96,768]{1,0:T(8,128)(2,1)S(1)}, u32[]{:S(2)}, u32[]{:S(2)}) collective-permute-start(bf16[96,768]{1,0:T(8,128)(2,1)S(1)} %get-tuple-element.80), channel_id=1, source_target_pairs={{1,2},{5,6},{9,10},{13,14},{17,18},{21,22},{25,26},{29,30},{2,1},{... | collective-permute-start | bytes 442376 | tf_op jit(solution)/shard_map/ppermute | solution.py:322
  57.2 14.3 %collective-permute-start.6 = (bf16[256,768]{1,0:T(8,128)(2,1)S(1)}, bf16[256,768]{1,0:T(8,128)(2,1)S(1)}, u32[]{:S(2)}, u32[]{:S(2)}) collective-permute-start(bf16[256,768]{1,0:T(8,128)(2,1)S(1)} %get-tuple-element.86), channel_id=1, source_target_pairs={{0,4},{1,5},{2,6},{3,7},{4,8},{5,9},{6,10},{7,11},{8,12},{9,13},{1... | collective-permute-start | bytes 1179656 | tf_op jit(solution)/shard_map/ppermute | solution.py:311
  60.1 9.3 %collective-permute-start.7 = (bf16[128,768]{1,0:T(8,128)(2,1)S(1)}, bf16[128,768]{1,0:T(8,128)(2,1)S(1)}, u32[]{:S(2)}, u32[]{:S(2)}) collective-permute-start(bf16[128,768]{1,0:T(8,128)(2,1)S(1)} %get-tuple-element.87), channel_id=1, source_target_pairs={{4,0},{5,1},{6,2},{7,3},{8,4},{9,5},{10,6},{11,7},{12,8},{13,9},{1... | collective-permute-start | bytes 589832 | tf_op jit(solution)/shard_map/ppermute | solution.py:311
  104.7 13.5 %copy-start.7 = (bf16[768,768]{1,0:T(8,128)(2,1)S(1)}, bf16[768,768]{1,0:T(8,128)(2,1)}, u32[]{:S(2)}) copy-start(bf16[768,768]{1,0:T(8,128)(2,1)} %refs_6_.3) | copy-start | bytes 3538948
  104.7 13.5 %copy-start.10 = (f32[768]{0:T(1024)S(1)}, f32[768]{0:T(1024)}, u32[]{:S(2)}) copy-start(f32[768]{0:T(1024)} %refs_7_.5) | copy-start | bytes 9220
  116.9 19.1 %collective-permute-start.10 = (bf16[256,768]{1,0:T(8,128)(2,1)S(1)}, bf16[256,768]{1,0:T(8,128)(2,1)S(1)}, u32[]{:S(2)}, u32[]{:S(2)}) collective-permute-start(bf16[256,768]{1,0:T(8,128)(2,1)S(1)} %bitcast.19), channel_id=1, source_target_pairs={{0,24},{1,25},{2,26},{3,27},{4,28},{5,29},{6,30},{7,31},{8,16},{9,... | collective-permute-start | bytes 1179656 | tf_op jit(solution)/shard_map/ppermute | solution.py:744
  118.0 18.0 %collective-permute-start.9 = (bf16[256,768]{1,0:T(8,128)(2,1)S(1)}, bf16[256,768]{1,0:T(8,128)(2,1)S(1)}, u32[]{:S(2)}, u32[]{:S(2)}) collective-permute-start(bf16[256,768]{1,0:T(8,128)(2,1)S(1)} %bitcast.20), channel_id=1, source_target_pairs={{0,8},{1,9},{2,10},{3,11},{4,12},{5,13},{6,14},{7,15},{8,0},{9,1},... | collective-permute-start | bytes 1179656 | tf_op jit(solution)/shard_map/ppermute | solution.py:744
  132.4 29.5 %collective-permute-start.8 = (bf16[256,768]{1,0:T(8,128)(2,1)S(1)}, bf16[256,768]{1,0:T(8,128)(2,1)S(1)}, u32[]{:S(2)}, u32[]{:S(2)}) collective-permute-start(bf16[256,768]{1,0:T(8,128)(2,1)S(1)} %bitcast.22), channel_id=1, source_target_pairs={{0,16},{1,17},{2,18},{3,19},{4,20},{5,21},{6,22},{7,23},{8,24},{9,... | collective-permute-start | bytes 1179656 | tf_op jit(solution)/shard_map/ppermute | solution.py:744
where the time goes:
time: 177 us; the launch traced here: 176 us
  Pallas kernels  90.6 us (51%)
  blocking collectives  55.4 us (31%)
  starting transfers between devices  21.2 us (12%)
  waiting for transfers between devices  6.93 us (4%)
  local copies, waits for them, and re-layouts  1.94 us (1%)
    pallas_call x3, Pallas kernels, attention(): pl.pallas_call(functools.partial(attention_kernel, steps), in_specs=[VM]...  54.5 us
    all_to_all x3, blocking collectives, everyones(): return lax.all_to_all(copies, 'tile', 0, 0, tiled=True)  44 us
    pallas_call x2, Pallas kernels, activate_inner(): pl.pallas_call(functools.partial(inner_kernel, before, after), grid=(rows...  13.4 us
    all_to_all x1, blocking collectives, query_slab(): lax.all_to_all(query, 'tile', 0, 0, tiled=True, axis_index_groups=groups)  11.3 us
    ppermute x4, starting transfers between devices, moved_by(): return lax.ppermute(value, 'tile', pairs)  11.2 us
    pallas_call x2, Pallas kernels, keys_values(): pl.pallas_call(kv_kernel, grid=(win // step,), in_specs=[pl.BlockSpec((st...  9.49 us
    ppermute x4, waiting for transfers between devices, moved_by(): return lax.ppermute(value, 'tile', pairs)  6.92 us
    pallas_call x1, Pallas kernels, mix0(): pl.pallas_call(functools.partial(mix0_kernel, cells, before, after), grid...  5.3 us
  transfers between devices with their start and end apart: 11, of which 2 were waited for; matrix products, arithmetic and copies ran while one was open for 0% of the time, Pallas kernels for 36%

commit v1 on v0

--- a/solution.py
+++ b/solution.py
@@ -16,7 +16,7 @@
 LOG2E = 1.4426950408889634
 QB = 256
 KC = 512
-UNROLL = {1: 4, 2: 8, 3: 8}
+UNROLL = {1: 8, 2: 8}
 
 
 def kv_kernel(x_ref, gain_ref, w_ref, b_ref, kt_ref, vt_ref):
@@ -351,7 +351,7 @@
             counted = jnp.sum(jnp.where(mine, g, 0.0).reshape(cols // 8, 8, 128), axis=0)
             return total + jnp.where((r >= own_rows[0]) & (r < own_rows[1]), counted, 0.0)
 
-        total = lax.fori_loop(0, rows, line, jnp.zeros((8, 128), F32), unroll=True)
+        total = lax.fori_loop(0, rows, line, jnp.zeros((8, 128), F32), unroll=5)
         total = jnp.sum(total, axis=0, keepdims=True)
         part_ref[:, group, :] += jnp.broadcast_to(total, (part_ref.shape[0], 128))
 

time: 177 us -> 177 us (level)
  no operation moved by 1% of the time
where the time goes in v1:
time: 177 us
  Pallas kernels  91.5 us (52%)
  blocking collectives  55.2 us (31%)
  starting transfers between devices  21.4 us (12%)
  waiting for transfers between devices  6.48 us (4%)
  local copies, waits for them, and re-layouts  1.94 us (1%)
    pallas_call x3, Pallas kernels, attention(): pl.pallas_call(functools.partial(attention_kernel, steps), in_specs=[VM]...  53.2 us
    all_to_all x3, blocking collectives, everyones(): return lax.all_to_all(copies, 'tile', 0, 0, tiled=True)  43.9 us
    pallas_call x2, Pallas kernels, activate_inner(): pl.pallas_call(functools.partial(inner_kernel, before, after), grid=(rows...  14.6 us
    all_to_all x1, blocking collectives, query_slab(): lax.all_to_all(query, 'tile', 0, 0, tiled=True, axis_index_groups=groups)  11.3 us
    ppermute x4, starting transfers between devices, moved_by(): return lax.ppermute(value, 'tile', pairs)  11.2 us
    pallas_call x2, Pallas kernels, keys_values(): pl.pallas_call(kv_kernel, grid=(win // step,), in_specs=[pl.BlockSpec((st...  9.49 us
    ppermute x4, waiting for transfers between devices, moved_by(): return lax.ppermute(value, 'tile', pairs)  6.46 us
    pallas_call x1, Pallas kernels, mix0(): pl.pallas_call(functools.partial(mix0_kernel, cells, before, after), grid...  5.3 us
  transfers between devices with their start and end apart: 11, of which 2 were waited for; matrix products, arithmetic and copies ran while one was open for 0% of the time, Pallas kernels for 36%

profile of v1, /device:TPU:0, one launch (start us, length us, event | category | flops | bytes accessed | tf_op | source)
XLA Modules:
  0.0 176.9 jit_solution(11842080327068839873)
XLA Ops:
  0.0 1.9 %copy-done = bf16[1,32,64,768]{3,2,1,0:T(8,128)(2,1)S(1)} copy-done((bf16[1,32,64,768]{3,2,1,0:T(8,128)(2,1)S(1)}, bf16[1,32,64,768]{3,2,1,0:T(8,128)(2,1)}, u32[]{:S(2)}) %copy-start) | copy-done | bytes 3145752
  1.9 0.2 side_pieces.1
  2.1 0.8 collective-permute-start.1
  2.9 3.6 %collective-permute-start = (bf16[64,768]{1,0:T(8,128)(2,1)S(1)}, bf16[64,768]{1,0:T(8,128)(2,1)S(1)}, u32[]{:S(2)}, u32[]{:S(2)}) collective-permute-start(bf16[64,768]{1,0:T(8,128)(2,1)S(1)} %get-tuple-element.57), channel_id=1, source_target_pairs={{0,1},{1,0},{2,3},{3,2},{4,5},{5,4},{6,7},{7,6},{8,9},{9,8},{10,11... | collective-permute-start | bytes 294920 | tf_op jit(solution)/shard_map/ppermute | solution.py:320
  6.5 4.7 %keys_values.2 = (bf16[6,1024,128]{2,1,0:T(8,128)(2,1)S(1)}, bf16[768,1024]{1,0:T(8,128)(2,1)S(1)}) custom-call(bf16[32,64,768]{2,1,0:T(8,128)(2,1)S(1)} %bitcast.6, f32[768]{0:T(1024)S(1)} %copy-done.9, bf16[768,1536]{1,0:T(8,128)(2,1)S(1)} %copy-done.6, f32[1536]{0:T(1024)S(1)} %copy-done.8), custom_call_target="tpu_custom_call" | custom-call | flops 4831838208 | bytes 8388608 | tf_op jit(solution)/shard_map/keys_values/pallas_call | solution.py:41
  11.2 0.1 line_pieces.2
  11.4 5.5 %collective-permute-start.2 = (bf16[144,768]{1,0:T(8,128)(2,1)S(1)}, bf16[144,768]{1,0:T(8,128)(2,1)S(1)}, u32[]{:S(2)}, u32[]{:S(2)}) collective-permute-start(bf16[144,768]{1,0:T(8,128)(2,1)S(1)} %get-tuple-element.64), channel_id=1, source_target_pairs={{0,4},{1,5},{2,6},{3,7},{4,8},{5,9},{6,10},{7,11},{8,12},{9,13},{1... | collective-permute-start | bytes 663560 | tf_op jit(solution)/shard_map/ppermute | solution.py:311
  16.9 1.3 collective-permute-start.3
  18.2 11.0 %activate_inner.2 = (f32[30,72,768]{2,1,0:T(8,128)S(1)}, bf16[30,72,768]{2,1,0:T(8,128)(2,1)S(1)}, f32[32,8,128]{2,1,0:T(8,128)S(1)}) custom-call(bf16[32,64,768]{2,1,0:T(8,128)(2,1)S(1)} %bitcast.9, bf16[64,768]{1,0:T(8,128)(2,1)S(1)} %collective-permute-done.rest_0_.l_ref, bf16[64,768]{1,0:T(8,128)(2,1)S(1)} %collective-permute-done.1.rest_1_.r_ref, ...), custom_call_target="tpu_custom_call" | custom-call | flops 663552000 | bytes 9953280 | tf_op jit(solution)/shard_map/activate_inner/pallas_call | solution.py:452
  29.3 1.5 activate_edge.2
  30.8 16.1 %all_to_all.20.sums = f32[32,8,128]{2,1,0:T(8,128)S(1)} all-to-all(f32[32,8,128]{2,1,0:T(8,128)S(1)} %get-tuple-element.73), channel_id=1, replica_groups=mesh['scene'=4,'tile'=32] {'tile'}, dimensions={0} | all-to-all | bytes 262144 | tf_op jit(solution)/shard_map/all_to_all | solution.py:677
  46.9 5.3 %mix0.1 = (bf16[16,32,768]{2,1,0:T(8,128)(2,1)S(1)}, bf16[96,768]{1,0:T(8,128)(2,1)S(1)}, bf16[96,768]{1,0:T(8,128)(2,1)S(1)}) custom-call(f32[32,8,128]{2,1,0:T(8,128)S(1)} %all_to_all.20.sums, bf16[3,192,768]{2,1,0:T(8,128)(2,1)S(1)} %bitcast.16, bf16[3,192,768]{2,1,0:T(8,128)(2,1)S(1)} %copy-done.4, bf16[3,768,768]{2,1,0:T(8,128)(2,1)S(1)} %copy-done.2, ...), custom_call_target="tpu_custom_call" | custom-call | flops 2548039680 | bytes 9953280 | tf_op jit(solution)/shard_map/mix0/pallas_call | solution.py:574
  52.2 0.2 collective-permute-start.4
  52.4 0.7 collective-permute-start.5
  53.1 4.7 %keys_values.3 = (bf16[6,1024,128]{2,1,0:T(8,128)(2,1)S(1)}, bf16[768,1024]{1,0:T(8,128)(2,1)S(1)}) custom-call(bf16[32,64,768]{2,1,0:T(8,128)(2,1)S(1)} %bitcast.12, f32[768]{0:T(1024)S(1)} %copy-done.9, bf16[768,1536]{1,0:T(8,128)(2,1)S(1)} %copy-done.6, f32[1536]{0:T(1024)S(1)} %copy-done.8), custom_call_target="tpu_custom_call" | custom-call | flops 4831838208 | bytes 8388608 | tf_op jit(solution)/shard_map/keys_values/pallas_call | solution.py:41
  57.8 0.2 line_pieces.3
  58.1 2.9 %collective-permute-start.6 = (bf16[256,768]{1,0:T(8,128)(2,1)S(1)}, bf16[256,768]{1,0:T(8,128)(2,1)S(1)}, u32[]{:S(2)}, u32[]{:S(2)}) collective-permute-start(bf16[256,768]{1,0:T(8,128)(2,1)S(1)} %get-tuple-element.86), channel_id=1, source_target_pairs={{0,4},{1,5},{2,6},{3,7},{4,8},{5,9},{6,10},{7,11},{8,12},{9,13},{1... | collective-permute-start | bytes 1179656 | tf_op jit(solution)/shard_map/ppermute | solution.py:311
  61.0 1.5 collective-permute-start.7
  62.5 3.6 %activate_inner.3 = (f32[14,40,768]{2,1,0:T(8,128)S(1)}, bf16[14,40,768]{2,1,0:T(8,128)(2,1)S(1)}, f32[32,8,128]{2,1,0:T(8,128)S(1)}) custom-call(bf16[16,32,768]{2,1,0:T(8,128)(2,1)S(1)} %get-tuple-element.88.top_ref.low_ref.x_ref, bf16[96,768]{1,0:T(8,128)(2,1)S(1)} %collective-permute-done.4.rest_0_.l_ref, ...), custom_call_target="tpu_custom_call" | custom-call | flops 172032000 | bytes 2580480 | tf_op jit(solution)/shard_map/activate_inner/pallas_call | solution.py:452
  66.1 4.2 %collective-permute-done.7.b_ref = bf16[128,768]{1,0:T(8,128)(2,1)S(1)} collective-permute-done((bf16[128,768]{1,0:T(8,128)(2,1)S(1)}, bf16[128,768]{1,0:T(8,128)(2,1)S(1)}, u32[]{:S(2)}, u32[]{:S(2)}) %collective-permute-start.7) | collective-permute-done | bytes 196640 | tf_op jit(solution)/shard_map/ppermute | solution.py:311
  70.3 2.2 %collective-permute-done.6.a_ref = bf16[256,768]{1,0:T(8,128)(2,1)S(1)} collective-permute-done((bf16[256,768]{1,0:T(8,128)(2,1)S(1)}, bf16[256,768]{1,0:T(8,128)(2,1)S(1)}, u32[]{:S(2)}, u32[]{:S(2)}) %collective-permute-start.6) | collective-permute-done | bytes 393248 | tf_op jit(solution)/shard_map/ppermute | solution.py:311
  72.5 2.3 %activate_edge.3 = (f32[9,40,768]{2,1,0:T(8,128)S(1)}, bf16[9,40,768]{2,1,0:T(8,128)(2,1)S(1)}, f32[32,8,128]{2,1,0:T(8,128)S(1)}) custom-call(bf16[16,32,768]{2,1,0:T(8,128)(2,1)S(1)} %get-tuple-element.88.top_ref.low_ref.x_ref, bf16[16,32,768]{2,1,0:T(8,128)(2,1)S(1)} %get-tuple-element.88.top_ref.low_ref.x_ref, ...), custom_call_target="tpu_custom_call" | custom-call | flops 110592000 | bytes 1658880 | tf_op jit(solution)/shard_map/activate_edge/pallas_call | solution.py:512
  74.8 16.6 %all_to_all.21.sums = f32[32,8,128]{2,1,0:T(8,128)S(1)} all-to-all(f32[32,8,128]{2,1,0:T(8,128)S(1)} %get-tuple-element.95), channel_id=1, replica_groups=mesh['scene'=4,'tile'=32] {'tile'}, dimensions={0} | all-to-all | bytes 262144 | tf_op jit(solution)/shard_map/all_to_all | solution.py:677
  91.4 3.6 %mix1.1 = (f32[9,24,768]{2,1,0:T(8,128)S(1)}, bf16[9,24,768]{2,1,0:T(8,128)(2,1)S(1)}, f32[32,8,128]{2,1,0:T(8,128)S(1)}) custom-call(f32[32,8,128]{2,1,0:T(8,128)S(1)} %all_to_all.21.sums, bf16[3,192,768]{2,1,0:T(8,128)(2,1)S(1)} %bitcast.17, bf16[3,192,768]{2,1,0:T(8,128)(2,1)S(1)} %copy-done.4, bf16[3,768,768]{2,1,0:T(8,128)(2,1)S(1)} %copy-done.2, ...), custom_call_target="tpu_custom_call" | custom-call | flops 1085276160 | bytes 4239360 | tf_op jit(solution)/shard_map/mix1/pallas_call | solution.py:628
  95.0 11.3 %all_to_all.22.sums = f32[32,8,128]{2,1,0:T(8,128)S(1)} all-to-all(f32[32,8,128]{2,1,0:T(8,128)S(1)} %get-tuple-element.100), channel_id=1, replica_groups=mesh['scene'=4,'tile'=32] {'tile'}, dimensions={0} | all-to-all | bytes 262144 | tf_op jit(solution)/shard_map/all_to_all | solution.py:677
  106.3 0.9 mix2.1
  107.2 11.3 %all_to_all.23 = bf16[8,32,768]{2,1,0:T(8,128)(2,1)S(1)} all-to-all(bf16[8,32,768]{2,1,0:T(8,128)(2,1)S(1)} %mix2.1), channel_id=1, replica_groups={{0,1,2,3,4,5,6,7},{8,9,10,11,12,13,14,15},{16,17,18,19,20,21,22,23},{24..., dimensions={0} | all-to-all | bytes 786432 | tf_op jit(solution)/shard_map/all_to_all | solution.py:718
  118.5 1.1 collective-permute-start.10
  119.8 13.6 %attention.3.refs_9_ = bf16[32,64,768]{2,1,0:T(8,128)(2,1)} custom-call(bf16[256,768]{1,0:T(8,128)(2,1)S(1)} %bitcast.21, bf16[6,1024,128]{2,1,0:T(8,128)(2,1)S(1)} %get-tuple-element.103.refs_1_.refs_2_, bf16[6,1024,128]{2,1,0:T(8,128)(2,1)S(1)} %get-tuple-element.104.refs_2_.refs_3_, bf16[768,1024]{1,0:T(8,128)(2,1)S(1)} %get-tuple-element.105.refs_3_.refs_4_, ...), custom_call_target="tpu_custom_call" | custom-call | flops 12884901888 | bytes 12582912 | tf_op jit(solution)/shard_map/attention/pallas_call | solution.py:153
  133.4 3.8 %collective-permute-start.8 = (bf16[256,768]{1,0:T(8,128)(2,1)S(1)}, bf16[256,768]{1,0:T(8,128)(2,1)S(1)}, u32[]{:S(2)}, u32[]{:S(2)}) collective-permute-start(bf16[256,768]{1,0:T(8,128)(2,1)S(1)} %bitcast.22), channel_id=1, source_target_pairs={{0,16},{1,17},{2,18},{3,19},{4,20},{5,21},{6,22},{7,23},{8,24},{9,... | collective-permute-start | bytes 1179656 | tf_op jit(solution)/shard_map/ppermute | solution.py:744
  137.2 26.0 %attention.4.refs_8_ = bf16[32,64,768]{2,1,0:T(8,128)(2,1)} custom-call(bf16[256,768]{1,0:T(8,128)(2,1)S(1)} %collective-permute-done.9.refs_0_, bf16[256,768]{1,0:T(8,128)(2,1)S(1)} %collective-permute-done.10.refs_1_, bf16[6,1024,128]{2,1,0:T(8,128)(2,1)S(1)} %get-tuple-element.103.refs_1_.refs_2_, ...), custom_call_target="tpu_custom_call", output_to_operand_aliasing={{}: (9, {})} | custom-call | flops 25769803776 | bytes 12582912 | tf_op jit(solution)/shard_map/attention/pallas_call | solution.py:153
  163.1 13.6 %attention.5 = bf16[32,64,768]{2,1,0:T(8,128)(2,1)} custom-call(bf16[256,768]{1,0:T(8,128)(2,1)S(1)} %collective-permute-done.8.refs_0_, bf16[6,1024,128]{2,1,0:T(8,128)(2,1)S(1)} %get-tuple-element.103.refs_1_.refs_2_, bf16[6,1024,128]{2,1,0:T(8,128)(2,1)S(1)} %get-tuple-element.104.refs_2_.refs_3_, ...), custom_call_target="tpu_custom_call", output_to_operand_aliasing={{}: (8, {})} | custom-call | flops 12884901888 | bytes 12582912 | tf_op jit(solution)/shard_map/attention/pallas_call | solution.py:153
  (31 shorter events, 0.2 us)
Async XLA Ops:
  0.0 1.9 %copy-start = (bf16[1,32,64,768]{3,2,1,0:T(8,128)(2,1)S(1)}, bf16[1,32,64,768]{3,2,1,0:T(8,128)(2,1)}, u32[]{:S(2)}) copy-start(bf16[1,32,64,768]{3,2,1,0:T(8,128)(2,1)} %param.10) | copy-start | bytes 9437188
  1.9 4.6 %copy-start.1 = (bf16[1,32,64,768]{3,2,1,0:T(8,128)(2,1)S(1)}, bf16[1,32,64,768]{3,2,1,0:T(8,128)(2,1)}, u32[]{:S(2)}) copy-start(bf16[1,32,64,768]{3,2,1,0:T(8,128)(2,1)} %param.10) | copy-start | bytes 9437188
  1.9 4.6 %copy-start.6 = (bf16[768,1536]{1,0:T(8,128)(2,1)S(1)}, bf16[768,1536]{1,0:T(8,128)(2,1)}, u32[]{:S(2)}) copy-start(bf16[768,1536]{1,0:T(8,128)(2,1)} %w_ref.3) | copy-start | bytes 7077892
  1.9 4.6 %copy-start.8 = (f32[1536]{0:T(1024)S(1)}, f32[1536]{0:T(1024)}, u32[]{:S(2)}) copy-start(f32[1536]{0:T(1024)} %b_ref.3) | copy-start | bytes 18436
  1.9 4.6 %copy-start.9 = (f32[768]{0:T(1024)S(1)}, f32[768]{0:T(1024)}, u32[]{:S(2)}) copy-start(f32[768]{0:T(1024)} %gain_ref.3) | copy-start | bytes 9220
  2.1 9.1 %collective-permute-start.1 = (bf16[64,768]{1,0:T(8,128)(2,1)S(1)}, bf16[64,768]{1,0:T(8,128)(2,1)S(1)}, u32[]{:S(2)}, u32[]{:S(2)}) collective-permute-start(bf16[64,768]{1,0:T(8,128)(2,1)S(1)} %get-tuple-element.58), channel_id=1, source_target_pairs={{1,2},{5,6},{9,10},{13,14},{17,18},{21,22},{25,26},{29,30},{2,1},{... | collective-permute-start | bytes 294920 | tf_op jit(solution)/shard_map/ppermute | solution.py:322
  2.9 8.3 %collective-permute-start = (bf16[64,768]{1,0:T(8,128)(2,1)S(1)}, bf16[64,768]{1,0:T(8,128)(2,1)S(1)}, u32[]{:S(2)}, u32[]{:S(2)}) collective-permute-start(bf16[64,768]{1,0:T(8,128)(2,1)S(1)} %get-tuple-element.57), channel_id=1, source_target_pairs={{0,1},{1,0},{2,3},{3,2},{4,5},{5,4},{6,7},{7,6},{8,9},{9,8},{10,11... | collective-permute-start | bytes 294920 | tf_op jit(solution)/shard_map/ppermute | solution.py:320
  11.2 6.9 %copy-start.5 = (bf16[3,3,3,768]{3,2,1,0:T(4,128)(2,1)S(1)}, bf16[3,3,3,768]{3,2,1,0:T(4,128)(2,1)}, u32[]{:S(2)}) copy-start(bf16[3,3,3,768]{3,2,1,0:T(4,128)(2,1)} %kernel.1) | copy-start | bytes 124420
  11.4 17.9 %collective-permute-start.2 = (bf16[144,768]{1,0:T(8,128)(2,1)S(1)}, bf16[144,768]{1,0:T(8,128)(2,1)S(1)}, u32[]{:S(2)}, u32[]{:S(2)}) collective-permute-start(bf16[144,768]{1,0:T(8,128)(2,1)S(1)} %get-tuple-element.64), channel_id=1, source_target_pairs={{0,4},{1,5},{2,6},{3,7},{4,8},{5,9},{6,10},{7,11},{8,12},{9,13},{1... | collective-permute-start | bytes 663560 | tf_op jit(solution)/shard_map/ppermute | solution.py:311
  16.9 12.4 %collective-permute-start.3 = (bf16[80,768]{1,0:T(8,128)(2,1)S(1)}, bf16[80,768]{1,0:T(8,128)(2,1)S(1)}, u32[]{:S(2)}, u32[]{:S(2)}) collective-permute-start(bf16[80,768]{1,0:T(8,128)(2,1)S(1)} %get-tuple-element.65), channel_id=1, source_target_pairs={{4,0},{5,1},{6,2},{7,3},{8,4},{9,5},{10,6},{11,7},{12,8},{13,9},{1... | collective-permute-start | bytes 368648 | tf_op jit(solution)/shard_map/ppermute | solution.py:311
  29.3 17.6 %copy-start.2 = (bf16[3,768,768]{2,1,0:T(8,128)(2,1)S(1)}, bf16[3,768,768]{2,1,0:T(8,128)(2,1)}, u32[]{:S(2)}) copy-start(bf16[3,768,768]{2,1,0:T(8,128)(2,1)} %mix.5) | copy-start | bytes 10616836
  29.3 17.6 %copy-start.3 = (bf16[3,768,192]{1,2,0:T(8,128)(2,1)S(1)}, bf16[3,768,192]{1,2,0:T(8,128)(2,1)}, u32[]{:S(2)}) copy-start(bf16[3,768,192]{1,2,0:T(8,128)(2,1)} %param.12) | copy-start | bytes 2654212
  29.3 17.6 %copy-start.4 = (bf16[3,192,768]{2,1,0:T(8,128)(2,1)S(1)}, bf16[3,192,768]{2,1,0:T(8,128)(2,1)}, u32[]{:S(2)}) copy-start(bf16[3,192,768]{2,1,0:T(8,128)(2,1)} %exp.5) | copy-start | bytes 2654212
  52.2 5.6 %collective-permute-start.4 = (bf16[96,768]{1,0:T(8,128)(2,1)S(1)}, bf16[96,768]{1,0:T(8,128)(2,1)S(1)}, u32[]{:S(2)}, u32[]{:S(2)}) collective-permute-start(bf16[96,768]{1,0:T(8,128)(2,1)S(1)} %get-tuple-element.79), channel_id=1, source_target_pairs={{0,1},{1,0},{2,3},{3,2},{4,5},{5,4},{6,7},{7,6},{8,9},{9,8},{10,11... | collective-permute-start | bytes 442376 | tf_op jit(solution)/shard_map/ppermute | solution.py:320
  52.4 5.4 %collective-permute-start.5 = (bf16[96,768]{1,0:T(8,128)(2,1)S(1)}, bf16[96,768]{1,0:T(8,128)(2,1)S(1)}, u32[]{:S(2)}, u32[]{:S(2)}) collective-permute-start(bf16[96,768]{1,0:T(8,128)(2,1)S(1)} %get-tuple-element.80), channel_id=1, source_target_pairs={{1,2},{5,6},{9,10},{13,14},{17,18},{21,22},{25,26},{29,30},{2,1},{... | collective-permute-start | bytes 442376 | tf_op jit(solution)/shard_map/ppermute | solution.py:322
  58.1 14.4 %collective-permute-start.6 = (bf16[256,768]{1,0:T(8,128)(2,1)S(1)}, bf16[256,768]{1,0:T(8,128)(2,1)S(1)}, u32[]{:S(2)}, u32[]{:S(2)}) collective-permute-start(bf16[256,768]{1,0:T(8,128)(2,1)S(1)} %get-tuple-element.86), channel_id=1, source_target_pairs={{0,4},{1,5},{2,6},{3,7},{4,8},{5,9},{6,10},{7,11},{8,12},{9,13},{1... | collective-permute-start | bytes 1179656 | tf_op jit(solution)/shard_map/ppermute | solution.py:311
  61.0 9.3 %collective-permute-start.7 = (bf16[128,768]{1,0:T(8,128)(2,1)S(1)}, bf16[128,768]{1,0:T(8,128)(2,1)S(1)}, u32[]{:S(2)}, u32[]{:S(2)}) collective-permute-start(bf16[128,768]{1,0:T(8,128)(2,1)S(1)} %get-tuple-element.87), channel_id=1, source_target_pairs={{4,0},{5,1},{6,2},{7,3},{8,4},{9,5},{10,6},{11,7},{12,8},{13,9},{1... | collective-permute-start | bytes 589832 | tf_op jit(solution)/shard_map/ppermute | solution.py:311
  106.3 13.5 %copy-start.7 = (bf16[768,768]{1,0:T(8,128)(2,1)S(1)}, bf16[768,768]{1,0:T(8,128)(2,1)}, u32[]{:S(2)}) copy-start(bf16[768,768]{1,0:T(8,128)(2,1)} %refs_6_.3) | copy-start | bytes 3538948
  106.3 13.5 %copy-start.10 = (f32[768]{0:T(1024)S(1)}, f32[768]{0:T(1024)}, u32[]{:S(2)}) copy-start(f32[768]{0:T(1024)} %refs_7_.5) | copy-start | bytes 9220
  118.5 18.6 %collective-permute-start.10 = (bf16[256,768]{1,0:T(8,128)(2,1)S(1)}, bf16[256,768]{1,0:T(8,128)(2,1)S(1)}, u32[]{:S(2)}, u32[]{:S(2)}) collective-permute-start(bf16[256,768]{1,0:T(8,128)(2,1)S(1)} %bitcast.19), channel_id=1, source_target_pairs={{0,24},{1,25},{2,26},{3,27},{4,28},{5,29},{6,30},{7,31},{8,16},{9,... | collective-permute-start | bytes 1179656 | tf_op jit(solution)/shard_map/ppermute | solution.py:744
  119.7 17.5 %collective-permute-start.9 = (bf16[256,768]{1,0:T(8,128)(2,1)S(1)}, bf16[256,768]{1,0:T(8,128)(2,1)S(1)}, u32[]{:S(2)}, u32[]{:S(2)}) collective-permute-start(bf16[256,768]{1,0:T(8,128)(2,1)S(1)} %bitcast.20), channel_id=1, source_target_pairs={{0,8},{1,9},{2,10},{3,11},{4,12},{5,13},{6,14},{7,15},{8,0},{9,1},... | collective-permute-start | bytes 1179656 | tf_op jit(solution)/shard_map/ppermute | solution.py:744
  133.4 29.7 %collective-permute-start.8 = (bf16[256,768]{1,0:T(8,128)(2,1)S(1)}, bf16[256,768]{1,0:T(8,128)(2,1)S(1)}, u32[]{:S(2)}, u32[]{:S(2)}) collective-permute-start(bf16[256,768]{1,0:T(8,128)(2,1)S(1)} %bitcast.22), channel_id=1, source_target_pairs={{0,16},{1,17},{2,18},{3,19},{4,20},{5,21},{6,22},{7,23},{8,24},{9,... | collective-permute-start | bytes 1179656 | tf_op jit(solution)/shard_map/ppermute | solution.py:744
